TPU v7x, 512 devices: a whole 4x4x16 slice. The times are simulated.
512 devices in a mesh: grp: 16 (over x, y), dev: 32 (over z, core).
Axes of the slice: x: 4, y: 4, z: 16, core: 2. Of those that a mesh axis runs over, the one named last changes fastest.
Arguments:
- records: bfloat16 [131072, 128], P('grp', 'dev')
- dropout: int32 [131072, 128], P('grp', 'dev'), may hold values 0 or 1
- counts: int32 [512], P(('grp', 'dev')), may hold values from 128 to 256, as said below
Outputs:
- upper: float32 [512, 512], replicated
- basis: bfloat16 [131072, 512], P(('grp', 'dev'))
Inputs may be any that keep to these rules, and one draw needn't show every extreme that they name: `counts`: at least one time shard has all 256 rows valid.
All inputs are finite; a program needn't handle non-finite values. No bound on the sum of `dropout` on one device may be relied on, other than what follows from the above.
Results may differ from a plain program's by a relative error of at most 0.0012.
Values may be sent and summed in bfloat16 or wider, within the bound.
No kernel may reach another device: no remote copies, remote signals or barrier semaphores. Data moves between devices by JAX's collectives and lax.ppermute only.
A program may use at most 128 MiB of HBM per device.

v0:
```python
import jax
import jax.numpy as jnp
from jax import lax
from jax.sharding import PartitionSpec as P

LAGS = 4


def from_behind(value, axis, by):
    size = lax.axis_size(axis)
    pairs = [(i, i + by) for i in range(size) if 0 <= i + by < size]
    return lax.ppermute(value, axis, pairs)


def gram_term(piece):
    return lax.dot_general(
        piece, piece, (((0,), (0,)), ((), ())), preferred_element_type=jnp.float32
    )


def project(piece, high, low):
    first = jnp.dot(piece, high, preferred_element_type=jnp.float32)
    second = jnp.dot(piece, low, preferred_element_type=jnp.float32)
    return (first + second).astype(jnp.bfloat16)


def exact_dot(left, right):
    return jnp.dot(left, right, precision=lax.Precision.HIGHEST)


def factor_block(block):
    size = block.shape[0]
    augmented = jnp.concatenate([block, jnp.eye(size, dtype=jnp.float32)], axis=1)
    order = jnp.arange(size, dtype=jnp.int32)

    def eliminate(step, state):
        working, written = state
        pivot_row = lax.dynamic_slice_in_dim(working, step, 1, 0)[0]
        pivot = lax.dynamic_slice_in_dim(pivot_row, step, 1, 0)[0]
        scaled = pivot_row / jnp.sqrt(pivot)
        column = lax.dynamic_slice_in_dim(working, step, 1, 1)[:, 0]
        factor = jnp.where(order > step, column / pivot, jnp.zeros_like(column))
        working = working - factor[:, None] * pivot_row[None, :]
        written = lax.dynamic_update_slice_in_dim(written, scaled[None, :], step, 0)
        return (working, written)

    _, written = lax.fori_loop(0, size, eliminate, (augmented, jnp.zeros_like(augmented)))
    upper_block = jnp.triu(written[:, :size])
    lower_inverse = jnp.tril(written[:, size:])
    return (upper_block, lower_inverse)


def factor_parts(matrix):
    size = matrix.shape[0]
    panel = min(128, size)
    panels = size // panel
    working = matrix
    diag_blocks = []
    diag_inverses = []
    right_blocks = []
    for number in range(panels):
        upper_block, lower_inverse = factor_block(working[:panel, :panel])
        beside = exact_dot(lower_inverse, working[:panel, panel:])
        working = working[panel:, panel:] - exact_dot(jnp.transpose(beside), beside)
        diag_blocks.append(upper_block)
        diag_inverses.append(jnp.transpose(lower_inverse))
        right_blocks.append(beside)
    block_rows = []
    for number in range(panels):
        pieces = []
        if number > 0:
            pieces.append(jnp.zeros((panel, number * panel), jnp.float32))
        pieces.append(diag_blocks[number])
        if number + 1 < panels:
            pieces.append(right_blocks[number])
        block_rows.append(jnp.concatenate(pieces, axis=1))
    upper = jnp.concatenate(block_rows, axis=0)
    solved = [[None] * panels for number in range(panels)]
    for column in range(panels):
        solved[column][column] = diag_inverses[column]
        for row in range(column - 1, -1, -1):
            accum = jnp.zeros((panel, panel), jnp.float32)
            for middle in range(row + 1, column + 1):
                coupling = upper[
                    row * panel : (row + 1) * panel, middle * panel : (middle + 1) * panel
                ]
                accum = accum + exact_dot(coupling, solved[middle][column])
            solved[row][column] = -exact_dot(diag_inverses[row], accum)
    inverse_rows = []
    for row in range(panels):
        pieces = []
        for column in range(panels):
            if column < row:
                pieces.append(jnp.zeros((panel, panel), jnp.float32))
            else:
                pieces.append(solved[row][column])
        inverse_rows.append(jnp.concatenate(pieces, axis=1))
    return (upper, jnp.concatenate(inverse_rows, axis=0))


def shards(records, dropout, counts):
    local = (records.astype(jnp.float32) * dropout.astype(jnp.float32)).astype(jnp.bfloat16)
    series = lax.all_to_all(local, "dev", split_axis=0, concat_axis=1, tiled=True)
    rows = series.shape[0]
    ahead = from_behind(series[: LAGS - 1], ("grp", "dev"), -1)
    padded = jnp.concatenate([series, ahead], axis=0)
    hankel = jnp.concatenate([padded[k : k + rows] for k in range(LAGS)], axis=1)
    valid = jnp.arange(rows, dtype=jnp.int32) >= rows - counts[0]
    hankel = jnp.where(valid[:, None], hankel, jnp.zeros_like(hankel))
    total_rows = rows * lax.axis_size("grp") * lax.axis_size("dev")
    partial_value = gram_term(hankel)
    gram = lax.psum(partial_value, ("grp", "dev"))
    upper, inverse = factor_parts(gram / total_rows)
    high = inverse.astype(jnp.bfloat16)
    low = (inverse - lax.optimization_barrier(high).astype(jnp.float32)).astype(jnp.bfloat16)
    basis = project(hankel, high, low)
    return (upper, basis)


def solution(mesh):
    in_specs = (P("grp", "dev"), P("grp", "dev"), P(("grp", "dev")))
    out_specs = (P(), P(("grp", "dev"), None))
    return jax.shard_map(shards, mesh=mesh, in_specs=in_specs, out_specs=out_specs, check_vma=False)
```

profile of v0, /device:TPU:1, one launch (start us, length us, event | category | flops | bytes accessed | tf_op | source)
XLA Modules:
  0.0 1999.9 jit_solution(4296532873974421739)
XLA Ops:
  7.2 1.6 multiply_convert_fusion
  8.7 16.8 all-to-all-start
  26.2 12.4 all-to-all-done
  38.6 3.5 collective-permute-start
  42.1 1.7 collective-permute-done
  44.0 1.3 fusion.66
  45.4 462.2 %all-reduce.3.cloned.1.call-done = f32[512,512]{1,0:T(8,128)} async-done(((f32[512,512]{1,0:T(8,128)}), f32[512,512]{1,0:T(8,128)}) %all-reduce.3.cloned.1.call-update) | async-done | bytes 1048592 | tf_op jit(solution)/shard_map/psum | solution.py:112
  507.6 1.3 broadcast_multiply_fusion
  509.1 368.6 %while.76 = (s32[]{:T(128)}, f32[128,256]{0,1:T(8,128)S(1)}, f32[128,256]{0,1:T(8,128)S(1)}, s32[]{:T(128)}, s32[]{:T(128)}, /*index=5*/s32[]{:T(128)}, s32[]{:T(128)}) while((s32[]{:T(128)}, f32[128,256]{0,1:T(8,128)S(1)}, f32[128,256]{0,1:T(8,128)S(1)}, s32[]{:T(128)}, s32[]{:T(128)}, /*index=5*/s32[]{:T(128)}, s32[]{:T(128)}) %tuple.188), condition=%wide.region_2.3_spmd.clone, body=%wide.region_1.2_spmd.clone.sunk | while | flops 66180 | bytes 271501 | solution.py:47
  513.9 0.7 fusion.92
  522.6 0.7 fusion.92
  531.2 0.7 fusion.92
  539.8 0.7 fusion.92
  542.7 0.7 fusion.92
  548.5 0.7 fusion.92
  551.4 0.7 fusion.92
  560.0 0.7 fusion.92
  568.7 0.7 fusion.92
  577.3 0.7 fusion.92
  585.9 0.7 fusion.92
  594.6 0.7 fusion.92
  597.5 0.7 fusion.92
  603.2 0.7 fusion.92
  606.1 0.7 fusion.92
  614.7 0.7 fusion.92
  623.4 0.7 fusion.92
  632.0 0.7 fusion.92
  640.7 0.7 fusion.92
  649.3 0.7 fusion.92
  652.2 0.7 fusion.92
  657.9 0.7 fusion.92
  660.8 0.7 fusion.92
  669.5 0.7 fusion.92
  678.1 0.7 fusion.92
  686.8 0.7 fusion.92
  695.4 0.7 fusion.92
  704.0 0.7 fusion.92
  706.9 0.7 fusion.92
  712.7 0.7 fusion.92
  715.6 0.7 fusion.92
  724.2 0.7 fusion.92
  732.8 0.7 fusion.92
  741.5 0.7 fusion.92
  750.1 0.7 fusion.92
  758.8 0.7 fusion.92
  761.6 0.7 fusion.92
  767.4 0.7 fusion.92
  770.3 0.7 fusion.92
  778.9 0.7 fusion.92
  787.6 0.7 fusion.92
  796.2 0.7 fusion.92
  804.9 0.7 fusion.92
  813.5 0.7 fusion.92
  816.4 0.7 fusion.92
  822.1 0.7 fusion.92
  825.0 0.7 fusion.92
  833.7 0.7 fusion.92
  842.3 0.7 fusion.92
  878.0 0.7 convolution_subtract_fusion
  878.9 368.6 %while.77 = (s32[]{:T(128)}, f32[128,256]{0,1:T(8,128)S(1)}, f32[128,256]{0,1:T(8,128)S(1)}, s32[]{:T(128)}, s32[]{:T(128)}, /*index=5*/s32[]{:T(128)}, s32[]{:T(128)}) while((s32[]{:T(128)}, f32[128,256]{0,1:T(8,128)S(1)}, f32[128,256]{0,1:T(8,128)S(1)}, s32[]{:T(128)}, s32[]{:T(128)}, /*index=5*/s32[]{:T(128)}, s32[]{:T(128)}) %tuple.191), condition=%wide.region_4.5_spmd.clone, body=%wide.region_3.4_spmd.clone.sunk | while | flops 66180 | bytes 271501 | solution.py:47
  1248.6 368.6 %while.78 = (s32[]{:T(128)}, f32[128,256]{0,1:T(8,128)S(1)}, f32[128,256]{0,1:T(8,128)S(1)}, s32[]{:T(128)}, s32[]{:T(128)}, /*index=5*/s32[]{:T(128)}, s32[]{:T(128)}) while((s32[]{:T(128)}, f32[128,256]{0,1:T(8,128)S(1)}, f32[128,256]{0,1:T(8,128)S(1)}, s32[]{:T(128)}, s32[]{:T(128)}, /*index=5*/s32[]{:T(128)}, s32[]{:T(128)}) %tuple.194), condition=%wide.region_6.7_spmd.clone, body=%wide.region_5.6_spmd.clone.sunk | while | flops 66180 | bytes 271501 | solution.py:47
  1618.2 368.6 %while.79 = (s32[]{:T(128)}, f32[128,256]{0,1:T(8,128)S(1)}, f32[128,256]{0,1:T(8,128)S(1)}, s32[]{:T(128)}, s32[]{:T(128)}, /*index=5*/s32[]{:T(128)}, s32[]{:T(128)}) while((s32[]{:T(128)}, f32[128,256]{0,1:T(8,128)S(1)}, f32[128,256]{0,1:T(8,128)S(1)}, s32[]{:T(128)}, s32[]{:T(128)}, /*index=5*/s32[]{:T(128)}, s32[]{:T(128)}) %tuple.197), condition=%wide.region_8.9_spmd.clone, body=%wide.region_7.8_spmd.clone.sunk | while | flops 66180 | bytes 271501 | solution.py:47
  1990.8 1.1 fusion.12
  1992.0 1.1 fusion.16
  (2569 shorter events, 1072.3 us)
Async XLA Ops:
  8.7 29.8 %all-to-all-start = ((bf16[32,256,4]{1,2,0:T(4,128)(2,1)}), bf16[32,256,4]{1,2,0:T(4,128)(2,1)S(1)}, u32[]{:S(2)}, u32[]{:S(2)}) async-start(bf16[32,256,4]{1,2,0:T(4,128)(2,1)} %bitcast.1), calls=%async_computation | async-start | bytes 131072 | tf_op jit(solution)/shard_map/all_to_all | solution.py:103
  25.5 482.1 %all-reduce.3.cloned.1.call-start = ((), (), s32[]{:S(2)}) async-start(), calls=%async_computation.1 | async-start | bytes 2097152 | tf_op jit(solution)/shard_map/psum | solution.py:112
  38.6 5.2 collective-permute-start
Sparse Core Ops, SparseCore 0:
  45.4 462.1 all-reduce.2
where the time goes:
time: 2020 us; the launch traced here: 2000 us
  local copies, waits for them, and re-layouts  614 us (30%)
  other arithmetic  489 us (24%)
  waiting for transfers between devices  476 us (24%)
  loops' own time  377 us (19%)
  starting transfers between devices  20.3 us (1%)
    psum x1, waiting for transfers between devices, shards(): gram = lax.psum(partial_value, ('grp', 'dev'))  462 us
    another operation x4, loops' own time, factor_block(): lax.fori_loop(0, size, eliminate, (augmented, jnp.zeros_like(augmented)))  377 us
    mul x512, other arithmetic, eliminate(): working = working - factor[:, None] * pivot_row[None, :]  337 us
    dynamic_update_slice x512, local copies, waits for them, and re-layouts, eliminate(): written = lax.dynamic_update_slice_in_dim(written, scaled[None, :], step, 0)  312 us
    dynamic_slice x512, local copies, waits for them, and re-layouts, eliminate(): pivot = lax.dynamic_slice_in_dim(pivot_row, step, 1, 0)[0]  301 us
    div x512, other arithmetic, eliminate(): scaled = pivot_row / jnp.sqrt(pivot)  94.6 us
    sub x512, other arithmetic, eliminate(): working = working - factor[:, None] * pivot_row[None, :]  53.9 us
  transfers between devices with their start and end apart: 3, of which 3 were waited for; matrix products, arithmetic and copies ran while one was open for 0% of the time, Pallas kernels for 0%

commit v1 on v0

--- a/solution.py
+++ b/solution.py
@@ -109,7 +109,7 @@
     hankel = jnp.where(valid[:, None], hankel, jnp.zeros_like(hankel))
     total_rows = rows * lax.axis_size("grp") * lax.axis_size("dev")
     partial_value = gram_term(hankel)
-    gram = lax.psum(partial_value, ("grp", "dev"))
+    gram = lax.psum(lax.psum(partial_value, "grp"), "dev")
     upper, inverse = factor_parts(gram / total_rows)
     high = inverse.astype(jnp.bfloat16)
     low = (inverse - lax.optimization_barrier(high).astype(jnp.float32)).astype(jnp.bfloat16)

time: 2020 us -> 1870 us (0.926)
  waiting for transfers between devices: 476 us -> 339 us
    psum x1 -> x2, waiting for transfers between devices: 462 us -> 325 us  [shards(): gram = lax.psum(lax.psum(partial_value, 'grp'), 'dev')]
  transfers between devices with their start and end apart: 3 -> 4, of which waited for: 3 -> 4; matrix products, arithmetic and copies ran while one was open for 0% -> 0% of each run, Pallas kernels for 0% -> 0%
where the time goes in v1:
time: 1870 us; the launch traced here: 1860 us
  local copies, waits for them, and re-layouts  618 us (33%)
  other arithmetic  484 us (26%)
  loops' own time  372 us (20%)
  waiting for transfers between devices  339 us (18%)
  starting transfers between devices  20.3 us (1%)
    another operation x4, loops' own time, factor_block(): lax.fori_loop(0, size, eliminate, (augmented, jnp.zeros_like(augmented)))  372 us
    mul x512, other arithmetic, eliminate(): working = working - factor[:, None] * pivot_row[None, :]  331 us
    psum x2, waiting for transfers between devices, shards(): gram = lax.psum(lax.psum(partial_value, 'grp'), 'dev')  325 us
    dynamic_update_slice x512, local copies, waits for them, and re-layouts, eliminate(): written = lax.dynamic_update_slice_in_dim(written, scaled[None, :], step, 0)  312 us
    dynamic_slice x512, local copies, waits for them, and re-layouts, eliminate(): pivot = lax.dynamic_slice_in_dim(pivot_row, step, 1, 0)[0]  305 us
    div x512, other arithmetic, eliminate(): scaled = pivot_row / jnp.sqrt(pivot)  94.6 us
    sub x512, other arithmetic, eliminate(): working = working - factor[:, None] * pivot_row[None, :]  53.9 us
  transfers between devices with their start and end apart: 4, of which 4 were waited for; matrix products, arithmetic and copies ran while one was open for 0% of the time, Pallas kernels for 0%

profile of v1, /device:TPU:1, one launch (start us, length us, event | category | flops | bytes accessed | tf_op | source)
XLA Modules:
  0.0 1856.3 jit_solution(7203295625269396698)
XLA Ops:
  7.2 1.6 multiply_convert_fusion
  8.7 16.8 all-to-all-start
  26.2 12.4 all-to-all-done
  38.6 3.5 collective-permute-start
  42.1 1.7 collective-permute-done
  44.0 1.3 fusion.66
  45.4 111.4 %all-reduce.4.cloned.1.call-done = f32[512,512]{1,0:T(8,128)} async-done(((f32[512,512]{1,0:T(8,128)}), f32[512,512]{1,0:T(8,128)}) %all-reduce.4.cloned.1.call-update) | async-done | bytes 1048592 | tf_op jit(solution)/shard_map/psum | solution.py:112
  156.8 213.3 %all-reduce.6.cloned.1.call-done = f32[512,512]{1,0:T(8,128)} async-done(((f32[512,512]{1,0:T(8,128)}), f32[512,512]{1,0:T(8,128)}) %all-reduce.6.cloned.1.call-update) | async-done | bytes 1048592 | tf_op jit(solution)/shard_map/psum | solution.py:112
  370.1 1.3 broadcast_multiply_fusion
  371.6 362.4 %while.76 = (s32[]{:T(128)}, f32[128,256]{0,1:T(8,128)S(1)}, f32[128,256]{0,1:T(8,128)S(1)}, s32[]{:T(128)}, s32[]{:T(128)}, /*index=5*/s32[]{:T(128)}, s32[]{:T(128)}) while((s32[]{:T(128)}, f32[128,256]{0,1:T(8,128)S(1)}, f32[128,256]{0,1:T(8,128)S(1)}, s32[]{:T(128)}, s32[]{:T(128)}, /*index=5*/s32[]{:T(128)}, s32[]{:T(128)}) %tuple.188), condition=%wide.region_3.4_spmd.clone, body=%wide.region_2.3_spmd.clone.sunk | while | flops 66180 | bytes 271501 | solution.py:47
  734.4 0.7 convolution_subtract_fusion
  735.2 368.6 %while.77 = (s32[]{:T(128)}, f32[128,256]{0,1:T(8,128)S(1)}, f32[128,256]{0,1:T(8,128)S(1)}, s32[]{:T(128)}, s32[]{:T(128)}, /*index=5*/s32[]{:T(128)}, s32[]{:T(128)}) while((s32[]{:T(128)}, f32[128,256]{0,1:T(8,128)S(1)}, f32[128,256]{0,1:T(8,128)S(1)}, s32[]{:T(128)}, s32[]{:T(128)}, /*index=5*/s32[]{:T(128)}, s32[]{:T(128)}) %tuple.191), condition=%wide.region_5.6_spmd.clone, body=%wide.region_4.5_spmd.clone.sunk | while | flops 66180 | bytes 271501 | solution.py:47
  737.2 0.7 fusion.93
  745.9 0.7 fusion.93
  751.6 0.7 fusion.93
  754.5 0.7 fusion.93
  760.3 0.7 fusion.93
  768.9 0.7 fusion.93
  777.6 0.7 fusion.93
  783.3 0.7 fusion.93
  792.0 0.7 fusion.93
  800.6 0.7 fusion.93
  806.4 0.7 fusion.93
  809.2 0.7 fusion.93
  815.0 0.7 fusion.93
  823.7 0.7 fusion.93
  832.3 0.7 fusion.93
  838.1 0.7 fusion.93
  846.7 0.7 fusion.93
  855.3 0.7 fusion.93
  861.1 0.7 fusion.93
  864.0 0.7 fusion.93
  869.7 0.7 fusion.93
  878.4 0.7 fusion.93
  887.0 0.7 fusion.93
  892.8 0.7 fusion.93
  901.4 0.7 fusion.93
  910.1 0.7 fusion.93
  915.8 0.7 fusion.93
  918.7 0.7 fusion.93
  924.5 0.7 fusion.93
  933.1 0.7 fusion.93
  941.8 0.7 fusion.93
  947.5 0.7 fusion.93
  956.2 0.7 fusion.93
  964.8 0.7 fusion.93
  970.6 0.7 fusion.93
  973.5 0.7 fusion.93
  979.2 0.7 fusion.93
  987.9 0.7 fusion.93
  996.5 0.7 fusion.93
  1002.3 0.7 fusion.93
  1010.9 0.7 fusion.93
  1019.6 0.7 fusion.93
  1025.3 0.7 fusion.93
  1028.2 0.7 fusion.93
  1034.0 0.7 fusion.93
  1042.6 0.7 fusion.93
  1051.3 0.7 fusion.93
  1057.0 0.7 fusion.93
  1105.0 368.6 %while.78 = (s32[]{:T(128)}, f32[128,256]{0,1:T(8,128)S(1)}, f32[128,256]{0,1:T(8,128)S(1)}, s32[]{:T(128)}, s32[]{:T(128)}, /*index=5*/s32[]{:T(128)}, s32[]{:T(128)}) while((s32[]{:T(128)}, f32[128,256]{0,1:T(8,128)S(1)}, f32[128,256]{0,1:T(8,128)S(1)}, s32[]{:T(128)}, s32[]{:T(128)}, /*index=5*/s32[]{:T(128)}, s32[]{:T(128)}) %tuple.194), condition=%wide.region_7.8_spmd.clone, body=%wide.region_6.7_spmd.clone.sunk | while | flops 66180 | bytes 271501 | solution.py:47
  1474.6 368.6 %while.79 = (s32[]{:T(128)}, f32[128,256]{0,1:T(8,128)S(1)}, f32[128,256]{0,1:T(8,128)S(1)}, s32[]{:T(128)}, s32[]{:T(128)}, /*index=5*/s32[]{:T(128)}, s32[]{:T(128)}) while((s32[]{:T(128)}, f32[128,256]{0,1:T(8,128)S(1)}, f32[128,256]{0,1:T(8,128)S(1)}, s32[]{:T(128)}, s32[]{:T(128)}, /*index=5*/s32[]{:T(128)}, s32[]{:T(128)}) %tuple.197), condition=%wide.region_9.10_spmd.clone, body=%wide.region_8.9_spmd.clone.sunk | while | flops 66180 | bytes 271501 | solution.py:47
  1847.2 1.1 fusion.12
  1848.4 1.1 fusion.16
  (2572 shorter events, 1071.8 us)
Async XLA Ops:
  8.7 29.8 %all-to-all-start = ((bf16[32,256,4]{1,2,0:T(4,128)(2,1)}), bf16[32,256,4]{1,2,0:T(4,128)(2,1)S(1)}, u32[]{:S(2)}, u32[]{:S(2)}) async-start(bf16[32,256,4]{1,2,0:T(4,128)(2,1)} %bitcast.1), calls=%async_computation | async-start | bytes 131072 | tf_op jit(solution)/shard_map/all_to_all | solution.py:103
  25.5 131.3 %all-reduce.4.cloned.1.call-start = ((), (), s32[]{:S(2)}) async-start(), calls=%async_computation.1 | async-start | bytes 2097152 | tf_op jit(solution)/shard_map/psum | solution.py:112
  38.6 5.2 collective-permute-start
  45.3 324.8 %all-reduce.6.cloned.1.call-start = ((), (), s32[]{:S(2)}) async-start(), calls=%async_computation.2 | async-start | bytes 2097152 | tf_op jit(solution)/shard_map/psum | solution.py:112
Sparse Core Ops, SparseCore 0:
  45.4 111.2 all-reduce.3
  159.1 210.9 all-reduce.5
